TPU v7x, 32 devices: a whole 2x2x4 slice. The times are simulated.
32 devices in a mesh: seq: 8 (over z, y), tp: 4 (over x, core).
Axes of the slice: x: 2, y: 2, z: 4, core: 2. Of those that a mesh axis runs over, the one named last changes fastest.
Arguments:
- patches: bfloat16 [4096, 1664], P('seq', 'tp'), may hold values from -30 to 30
- grad_merged: bfloat16 [1024, 1664], P('seq', 'tp'), may hold values from -6 to 6
- norm_gain: float32 [1664], replicated, may hold values from 0.25 to 1.75
- qkv_weight: bfloat16 [1664, 2496], P(None, 'tp'), may hold values from -0.15625 to 0.15625
- proj_weight: bfloat16 [832, 1664], P('tp'), may hold values from -0.21875 to 0.21875
- grid_height: int32 [24], replicated, may hold values from 4 to 8
- grid_width: int32 [24], replicated, may hold values from 3 to 5, as said below
Outputs:
- patch_grad: bfloat16 [4096, 1664], P('seq', 'tp')
- qkv_grad: float32 [1664, 2496], P('seq', 'tp')
Inputs may be any that keep to these rules, and one draw needn't show every extreme that they name: `grid_width`: the merged rows of one shard's three images add up to at most 120, exactly that on some shard.
All inputs are finite; a program needn't handle non-finite values.
Results may differ from a plain program's by a relative error of at most 0.011.
Values may be sent and summed in bfloat16 or wider, within the bound.
A program may use at most 64 MiB of HBM per device.

v0:
```python
import jax
import jax.numpy as jnp
from jax import lax
from jax.sharding import PartitionSpec as P

HEAD_SIZE = 104


soft_cap = 5.0
norm_eps = 1e-06


def stream_bounds(grid_height, grid_width, shard_count):
    image_sizes = grid_height * grid_width
    image_ends = jnp.cumsum(image_sizes)
    image_shard = jnp.arange(image_sizes.shape[0], dtype=jnp.int32) // 3
    owner_ids = jnp.arange(shard_count, dtype=jnp.int32)
    shard_load = jnp.sum(
        jnp.where(image_shard[None, :] == owner_ids[:, None], image_sizes[None, :], 0), axis=1
    )
    first_row = jnp.sum(
        jnp.where(image_shard[None, :] < owner_ids[:, None], image_sizes[None, :], 0), axis=1
    )
    return (image_ends, first_row, shard_load)


def pooled(window_rows, feat_width):
    summed = window_rows.reshape(-1, 4, feat_width).astype(jnp.float32).sum(axis=1)
    return (summed * 0.25).astype(jnp.bfloat16)


def on_device(patches, grad_merged, norm_gain, qkv_weight, proj_weight, grid_height, grid_width):
    shard_count = lax.axis_size("seq")
    myself = lax.axis_index("seq")
    tp_index = lax.axis_index("tp")
    row_count = grad_merged.shape[0]
    feat_width = grad_merged.shape[1]
    slot_count = -(-row_count // shard_count)
    slot_total = shard_count * slot_count
    image_ends, first_row, shard_load = stream_bounds(grid_height, grid_width, shard_count)
    stream_total = image_ends[-1]
    slot_ids = jnp.arange(slot_count, dtype=jnp.int32)
    owner_ids = jnp.arange(shard_count, dtype=jnp.int32)
    lead_row = (first_row - myself + shard_count - 1) // shard_count
    placed = lead_row[:, None] + slot_ids[None, :]
    sending = (placed * shard_count + myself < (first_row + shard_load)[:, None]) & (
        placed < row_count
    )
    picked = jnp.minimum(placed, row_count - 1).reshape(-1)

    def outgoing(source_rows):
        chosen = source_rows[picked].reshape(shard_count, slot_count, source_rows.shape[1])
        return jnp.where(sending[:, :, None], chosen, 0)

    windows = patches.reshape(row_count, 4 * feat_width)
    arrived_win, arrived_grad = (
        lax.all_to_all(outgoing(windows), "seq", split_axis=0, concat_axis=0, tiled=True),
        lax.all_to_all(outgoing(grad_merged), "seq", split_axis=0, concat_axis=0, tiled=True),
    )
    arrived = pooled(arrived_win.reshape(slot_total, 4 * feat_width), feat_width)
    arrived_grad = arrived_grad.reshape(slot_total, feat_width)
    row_values, row_grads = (
        lax.all_gather(arrived, "tp", axis=1, tiled=True),
        lax.all_gather(arrived_grad, "tp", axis=1, tiled=True),
    )
    first_here = first_row[myself]
    end_here = first_here + shard_load[myself]
    stream_in = (
        ((first_here - owner_ids + shard_count - 1) // shard_count)[:, None] + slot_ids[None, :]
    ) * shard_count + owner_ids[:, None]
    stream_in = stream_in.reshape(-1)
    live = stream_in < end_here
    image_index = jnp.sum(image_ends[None, :] <= stream_in[:, None], axis=1)
    image_key = jnp.where(live, image_index, -1 - jnp.arange(slot_total, dtype=jnp.int32))
    same_image = image_key[:, None] == image_key[None, :]
    values_f32 = row_values.astype(jnp.float32)
    inv_rms = lax.rsqrt(jnp.mean(values_f32 * values_f32, axis=-1, keepdims=True) + norm_eps)
    unit_rows = values_f32 * inv_rms
    normed = (unit_rows * norm_gain).astype(jnp.bfloat16)
    head_count = qkv_weight.shape[1] // (3 * HEAD_SIZE)
    packed = jnp.dot(normed, qkv_weight, preferred_element_type=jnp.float32).astype(jnp.bfloat16)
    packed = packed.reshape(slot_total, head_count, 3, HEAD_SIZE)
    queries = packed[:, :, 0]
    key_rows = packed[:, :, 1]
    values = packed[:, :, 2]
    score_scale = HEAD_SIZE ** (-0.5)
    logits = (
        jnp.einsum("qhe,khe->hqk", queries, key_rows, preferred_element_type=jnp.float32)
        * score_scale
    )
    capped = jnp.tanh(logits * (1.0 / soft_cap))
    raised = jnp.where(same_image[None], jnp.exp(soft_cap * capped), 0.0)
    attn_probs = raised / jnp.sum(raised, axis=-1, keepdims=True)
    probs_half = attn_probs.astype(jnp.bfloat16)
    grad_heads = jnp.einsum(
        "rd,cd->rc", row_grads, proj_weight, preferred_element_type=jnp.float32
    ).astype(jnp.bfloat16)
    grad_heads = grad_heads.reshape(slot_total, head_count, HEAD_SIZE)
    grad_prob = jnp.einsum("qhe,khe->hqk", grad_heads, values, preferred_element_type=jnp.float32)
    grad_score = attn_probs * (grad_prob - jnp.sum(attn_probs * grad_prob, axis=-1, keepdims=True))
    grad_logit = (grad_score * (1.0 - capped * capped)).astype(jnp.bfloat16)
    grad_query = (
        jnp.einsum("hqk,khe->qhe", grad_logit, key_rows, preferred_element_type=jnp.float32)
        * score_scale
    ).astype(jnp.bfloat16)
    grad_key = (
        jnp.einsum("hqk,qhe->khe", grad_logit, queries, preferred_element_type=jnp.float32)
        * score_scale
    ).astype(jnp.bfloat16)
    grad_value = jnp.einsum(
        "hqk,qhe->khe", probs_half, grad_heads, preferred_element_type=jnp.float32
    ).astype(jnp.bfloat16)
    grad_cols = jnp.stack([grad_query, grad_key, grad_value], axis=2).reshape(
        slot_total, 3 * head_count * HEAD_SIZE
    )
    head_part = jnp.einsum("rc,dc->rd", grad_cols, qkv_weight, preferred_element_type=jnp.float32)
    grad_normed = lax.psum(head_part, "tp")
    scaled = grad_normed * norm_gain
    grad_rows = inv_rms * (
        scaled - unit_rows * jnp.mean(scaled * unit_rows, axis=-1, keepdims=True)
    ) + row_grads.astype(jnp.float32)
    grad_rows = jnp.where(live[:, None], grad_rows, 0.0).astype(jnp.bfloat16)
    own_cols = lax.dynamic_slice_in_dim(grad_rows, tp_index * feat_width, feat_width, 1)
    local_rows = jnp.arange(row_count, dtype=jnp.int32)
    stream_out = local_rows * shard_count + myself
    owner_of = jnp.sum((first_row + shard_load)[None, :] <= stream_out[:, None], axis=1)
    owner_safe = jnp.minimum(owner_of, shard_count - 1)
    valid_out = stream_out < stream_total
    flat_out = jnp.clip(
        owner_safe * slot_count + local_rows - lead_row[owner_safe], 0, slot_total - 1
    )
    quarter = jnp.broadcast_to((own_cols * 0.25)[:, None, :], (slot_total, 4, feat_width))
    returned = lax.all_to_all(
        quarter.reshape(shard_count, slot_count, 4 * feat_width),
        "seq",
        split_axis=0,
        concat_axis=0,
        tiled=True,
    )
    windows_back = returned.reshape(slot_total, 4 * feat_width)[flat_out]
    windows_back = jnp.where(valid_out[:, None], windows_back, 0)
    patch_grad = windows_back.reshape(4 * row_count, feat_width)
    qkv_sum = lax.psum_scatter(
        jnp.einsum("rd,rc->dc", normed, grad_cols, preferred_element_type=jnp.float32),
        "seq",
        scatter_dimension=0,
        tiled=True,
    )
    qkv_grad = qkv_sum * (row_count * shard_count) ** (-0.5)
    return (patch_grad, qkv_grad)


def solution(mesh):
    in_specs = (P("seq", "tp"), P("seq", "tp"), P(), P(None, "tp"), P("tp", None), P(), P())
    out_specs = (P("seq", "tp"), P("seq", "tp"))
    return jax.shard_map(
        on_device, mesh=mesh, in_specs=in_specs, out_specs=out_specs, check_vma=False
    )
```

profile of v0, /device:TPU:0, one launch (start us, length us, event | category | flops | bytes accessed | tf_op | source)
XLA Modules:
  0.0 169.3 jit_solution(12615541140282880816)
XLA Ops:
  8.0 0.8 mul.150
  9.0 0.7 dynamic_slice.9
  9.7 0.7 fusion.47
  10.7 1.0 copy.94
  11.7 0.8 gather_fusion.1
  12.5 0.7 broadcast_select_fusion.2
  13.3 7.3 %all-to-all-start.1 = ((bf16[8,16,416]{2,1,0:T(8,128)(2,1)}), bf16[8,16,416]{2,1,0:T(8,128)(2,1)S(1)}, u32[]{:S(2)}, u32[]{:S(2)}) async-start(bf16[8,16,416]{2,1,0:T(8,128)(2,1)} %broadcast_select_fusion.2), calls=%async_computation.1 | async-start | bytes 262144 | tf_op jit(solution)/shard_map/all_to_all | solution.py:58
  20.6 0.2 copy.89
  20.8 0.6 reshape.362
  21.4 1.0 gather_fusion
  22.4 0.9 broadcast_select_fusion.1
  23.3 0.6 dynamic_slice.10
  25.6 2.3 %all-to-all-done.1 = bf16[8,16,416]{2,1,0:T(8,128)(2,1)S(1)} async-done(((bf16[8,16,416]{2,1,0:T(8,128)(2,1)}), bf16[8,16,416]{2,1,0:T(8,128)(2,1)S(1)}, u32[]{:S(2)}, u32[]{:S(2)}) %all-to-all-start.1) | async-done | bytes 106528 | tf_op jit(solution)/shard_map/all_to_all | solution.py:58
  27.9 4.1 %all-to-all-start = ((bf16[8,16,1664]{2,1,0:T(8,128)(2,1)}), bf16[8,16,1664]{2,1,0:T(8,128)(2,1)}, u32[]{:S(2)}, u32[]{:S(2)}) async-start(bf16[8,16,1664]{2,1,0:T(8,128)(2,1)} %broadcast_select_fusion.1), calls=%async_computation | async-start | bytes 851968 | tf_op jit(solution)/shard_map/all_to_all | solution.py:57
  32.1 0.5 subtract_select_fusion
  32.6 0.7 broadcast_compare_fusion
  33.4 6.6 %all_gather.7 = bf16[128,1664]{0,1:T(8,128)(2,1)S(1)} all-gather(bf16[128,416]{0,1:T(8,128)(2,1)S(1)} %copy.95), channel_id=1, replica_groups=mesh['seq'=8,'tp'=4] {'tp'}, dimensions={1}, use_global_device_ids=true | all-gather | bytes 532480 | tf_op jit(solution)/shard_map/all_gather | solution.py:64
  40.0 1.0 convolution_convert_fusion.1
  41.0 2.5 %all-to-all-done = bf16[8,16,1664]{2,1,0:T(8,128)(2,1)} async-done(((bf16[8,16,1664]{2,1,0:T(8,128)(2,1)}), bf16[8,16,1664]{2,1,0:T(8,128)(2,1)}, u32[]{:S(2)}, u32[]{:S(2)}) %all-to-all-start) | async-done | bytes 426016 | tf_op jit(solution)/shard_map/all_to_all | solution.py:57
  43.5 2.1 %reshape.371 = f32[128,4,416]{2,1,0:T(4,128)S(1)} reshape(bf16[8,16,1664]{2,1,0:T(8,128)(2,1)} %all-to-all-done) | data formatting | bytes 1277952 | tf_op jit(solution)/shard_map/convert_element_type | solution.py:28
  45.6 1.4 reduce_sum.83
  47.0 1.1 copy.90
  48.2 6.6 %all_gather.6 = bf16[128,1664]{0,1:T(8,128)(2,1)S(1)} all-gather(bf16[128,416]{0,1:T(8,128)(2,1)S(1)} %multiply_convert_fusion.1), channel_id=1, replica_groups=mesh['seq'=8,'tp'=4] {'tp'}, dimensions={1}, use_global_device_ids=true | all-gather | bytes 532480 | tf_op jit(solution)/shard_map/all_gather | solution.py:63
  54.8 0.3 copy.91
  55.1 0.2 fusion.11
  55.3 0.8 convolution_convert_fusion
  56.1 0.2 fusion.27
  56.3 0.9 fusion.23
  57.2 1.1 fusion.8
  58.3 1.2 fusion.9
  59.5 1.2 fusion.10
  60.8 1.5 fusion.48
  62.4 2.8 %fusion.20 = f32[1664,624]{1,0:T(8,128)} fusion(bf16[128,624]{0,1:T(8,128)(2,1)S(1)} %bitcast.100, f32[1664]{0:T(1024)S(1)} %copy-done.4, bf16[128,1664]{1,0:T(8,128)(2,1)S(1)} %copy.91, f32[128]{0:T(128)S(1)} %add_rsqrt_fusion), kind=kOutput, calls=%fused_computation.40 | convolution fusion | flops 266665984 | bytes 4746240 | tf_op jit(solution)/shard_map/rd,rc->dc/dot_general | solution.py:144
  65.2 1.2 slice.32
  66.5 29.9 %all-reduce.2.cloned.1.call-done = f32[128,1664]{1,0:T(8,128)} async-done(((f32[128,1664]{1,0:T(8,128)}), f32[128,1664]{1,0:T(8,128)}) %all-reduce.2.cloned.1.call-update) | async-done | bytes 851984 | tf_op jit(solution)/shard_map/psum | solution.py:117
  96.4 1.4 multiply_reduce_fusion
  97.9 0.3 fusion.21
  98.3 1.3 reshape.369
  99.6 5.5 %all-to-all-start.2 = ((bf16[8,16,1664]{2,1,0:T(8,128)(2,1)}), bf16[8,16,1664]{2,1,0:T(8,128)(2,1)S(1)}, u32[]{:S(2)}, u32[]{:S(2)}) async-start(bf16[8,16,1664]{2,1,0:T(8,128)(2,1)} %reshape.369), calls=%async_computation.2 | async-start | bytes 851968 | tf_op jit(solution)/shard_map/all_to_all | solution.py:133
  105.1 0.7 broadcast_compare_fusion.2
  105.9 0.7 fusion.46
  106.7 5.0 %fusion.35 = s32[128]{0:T(128)S(1)} fusion(s32[128]{0:T(128)S(1)} %convert_reduce_fusion.1, s32[]{:T(128)} %bitcast.24, s32[]{:T(128)} %bitcast.25, s32[]{:T(128)} %bitcast.26, s32[]{:T(128)} %bitcast.27, s32[]{:T(128)} %bitcast.28, s32[]{:T(128)} %bitcast.30, s32[]{:T(128)} %bitcast.29, s32[]{:T(128)} %bitcast.23), kind=kLoop, calls=%fused_computation.96 | loop fusion | flops 3200 | bytes 1056 | tf_op jit(solution)/shard_map/select_n | solution.py:140
  111.7 7.7 %all-to-all-done.2 = bf16[8,16,1664]{2,1,0:T(8,128)(2,1)S(1)} async-done(((bf16[8,16,1664]{2,1,0:T(8,128)(2,1)}), bf16[8,16,1664]{2,1,0:T(8,128)(2,1)S(1)}, u32[]{:S(2)}, u32[]{:S(2)}) %all-to-all-start.2) | async-done | bytes 426016 | tf_op jit(solution)/shard_map/all_to_all | solution.py:133
  119.4 0.9 gather_fusion.2
  120.3 0.6 gather.21
  121.1 0.9 copy.102
  122.0 38.0 %reduce-scatter.2.cloned.1.call-done = f32[208,624]{1,0:T(8,128)} async-done(((f32[1664,624]{1,0:T(8,128)}), f32[208,624]{1,0:T(8,128)}) %reduce-scatter.2.cloned.1.call-update) | async-done | bytes 519184 | tf_op jit(solution)/shard_map/reduce_scatter | solution.py:143
  160.0 1.9 %broadcast_multiply_fusion.1 = f32[208,624]{1,0:T(8,128)} fusion(f32[208,624]{1,0:T(8,128)} %reduce-scatter.2.cloned.1.call-done), kind=kLoop, calls=%fused_computation.28 | loop fusion | flops 129792 | bytes 1038336 | tf_op jit(solution)/shard_map/mul | solution.py:149
  (52 shorter events, 1.9 us)
Async XLA Ops:
  8.0 47.2 %copy-start = (bf16[1664,624]{0,1:T(8,128)(2,1)S(1)}, bf16[1664,624]{0,1:T(8,128)(2,1)}, u32[]{:S(2)}) copy-start(bf16[1664,624]{0,1:T(8,128)(2,1)} %param.10) | copy-start | bytes 6230020
  8.0 12.5 %copy-start.2 = (bf16[512,416]{0,1:T(8,128)(2,1)S(1)}, bf16[512,416]{0,1:T(8,128)(2,1)}, u32[]{:S(2)}) copy-start(bf16[512,416]{0,1:T(8,128)(2,1)} %param.7) | copy-start | bytes 1277956
  10.4 12.0 %copy-start.8 = (s32[8]{0:T(128)}, s32[8]{0:T(128)S(1)}, u32[]{:S(2)}) copy-start(s32[8]{0:T(128)S(1)} %get-tuple-element.29) | copy-start | bytes 100
  13.3 14.6 %all-to-all-start.1 = ((bf16[8,16,416]{2,1,0:T(8,128)(2,1)}), bf16[8,16,416]{2,1,0:T(8,128)(2,1)S(1)}, u32[]{:S(2)}, u32[]{:S(2)}) async-start(bf16[8,16,416]{2,1,0:T(8,128)(2,1)} %broadcast_select_fusion.2), calls=%async_computation.1 | async-start | bytes 262144 | tf_op jit(solution)/shard_map/all_to_all | solution.py:58
  22.4 17.7 %copy-start.1 = (bf16[208,1664]{1,0:T(8,128)(2,1)S(1)}, bf16[208,1664]{1,0:T(8,128)(2,1)}, u32[]{:S(2)}) copy-start(bf16[208,1664]{1,0:T(8,128)(2,1)} %param.11) | copy-start | bytes 2076676
  25.4 7.9 %copy-start.5 = (s32[24,1]{1,0:T(8,128)}, s32[24,1]{1,0:T(8,128)S(1)}, u32[]{:S(2)}) copy-start(s32[24,1]{1,0:T(8,128)S(1)} %reduce-window.4) | copy-start | bytes 292
  27.9 15.6 %all-to-all-start = ((bf16[8,16,1664]{2,1,0:T(8,128)(2,1)}), bf16[8,16,1664]{2,1,0:T(8,128)(2,1)}, u32[]{:S(2)}, u32[]{:S(2)}) async-start(bf16[8,16,1664]{2,1,0:T(8,128)(2,1)} %broadcast_select_fusion.1), calls=%async_computation | async-start | bytes 851968 | tf_op jit(solution)/shard_map/all_to_all | solution.py:57
  32.0 64.4 %all-reduce.2.cloned.1.call-start = ((), (), s32[]{:S(2)}) async-start(), calls=%async_computation.4 | async-start | bytes 1703936 | tf_op jit(solution)/shard_map/psum | solution.py:117
  47.0 8.2 %copy-start.4 = (f32[1664]{0:T(1024)S(1)}, f32[1664]{0:T(1024)}, u32[]{:S(2)}) copy-start(f32[1664]{0:T(1024)} %param.9) | copy-start | bytes 19972
  54.8 1.3 copy-start.3
  54.8 1.5 copy-start.6
  62.3 97.7 %reduce-scatter.2.cloned.1.call-start = ((), (), s32[]{:S(2)}) async-start(), calls=%async_computation.5 | async-start | bytes 4792320 | tf_op jit(solution)/shard_map/reduce_scatter | solution.py:143
  65.2 32.7 %copy-start.7 = (pred[128]{0:T(512)(128)(4,1)S(1)}, pred[128]{0:T(512)(128)(4,1)}, u32[]{:S(2)}) copy-start(pred[128]{0:T(512)(128)(4,1)} %get-tuple-element.19) | copy-start | bytes 388
  97.9 8.7 %copy-start.9 = (s32[8]{0:T(128)S(1)}, s32[8]{0:T(128)}, u32[]{:S(2)}) copy-start(s32[8]{0:T(128)} %copy-done.8) | copy-start | bytes 100
  99.6 19.8 %all-to-all-start.2 = ((bf16[8,16,1664]{2,1,0:T(8,128)(2,1)}), bf16[8,16,1664]{2,1,0:T(8,128)(2,1)S(1)}, u32[]{:S(2)}, u32[]{:S(2)}) async-start(bf16[8,16,1664]{2,1,0:T(8,128)(2,1)} %reshape.369), calls=%async_computation.2 | async-start | bytes 851968 | tf_op jit(solution)/shard_map/all_to_all | solution.py:133
Sparse Core Ops, SparseCore 0:
  62.4 33.9 all-reduce.1
Sparse Core Ops, SparseCore 1:
  66.8 93.1 reduce-scatter.1
where the time goes:
time: 170 us; the launch traced here: 169 us
  waiting for transfers between devices  80.5 us (47%)
  starting transfers between devices  17 us (10%)
  between operations  17 us (10%)
  other arithmetic  16.1 us (9%)
  local copies, waits for them, and re-layouts  14.8 us (9%)
  blocking collectives  13.3 us (8%)
  matrix products  10.7 us (6%)
    reduce_scatter x1, waiting for transfers between devices, on_device(): lax.psum_scatter(jnp.einsum('rd,rc->dc', normed, grad_cols, preferred_ele...  38 us
    psum x1, waiting for transfers between devices, on_device(): grad_normed = lax.psum(head_part, 'tp')  29.9 us
    all_to_all x1, waiting for transfers between devices, on_device(): lax.all_to_all(quarter.reshape(shard_count, slot_count, 4 * feat_width),...  7.67 us
    all_to_all x1, starting transfers between devices, on_device(): lax.all_to_all(outgoing(grad_merged), 'seq', split_axis=0, concat_axis=0,...  7.28 us
    all_gather x1, blocking collectives, on_device(): lax.all_gather(arrived_grad, 'tp', axis=1, tiled=True)  6.64 us
    all_gather x1, blocking collectives, on_device(): lax.all_gather(arrived, 'tp', axis=1, tiled=True)  6.64 us
    all_to_all x1, starting transfers between devices, on_device(): lax.all_to_all(quarter.reshape(shard_count, slot_count, 4 * feat_width),...  5.48 us
    select_n x1, other arithmetic, on_device(): windows_back = returned.reshape(slot_total, 4 * feat_width)[flat_out]  4.98 us
  transfers between devices with their start and end apart: 5, of which 5 were waited for; matrix products, arithmetic and copies ran while one was open for 13% of the time, Pallas kernels for 0%

commit v1 on v0

--- a/solution.py
+++ b/solution.py
@@ -1,6 +1,10 @@
+import functools
+
 import jax
 import jax.numpy as jnp
 from jax import lax
+from jax.experimental import pallas as pl
+from jax.experimental.pallas import tpu as pltpu
 from jax.sharding import PartitionSpec as P
 
 HEAD_SIZE = 104
@@ -150,9 +154,412 @@
     return (patch_grad, qkv_grad)
 
 
+MESH = pl.DeviceIdType.MESH
+NT = (((1,), (1,)), ((), ()))
+TN = (((0,), (0,)), ((), ()))
+BF = jnp.bfloat16
+F32 = jnp.float32
+
+
+def mm(a, b, dims=(((1,), (0,)), ((), ()))):
+    return lax.dot_general(a, b, dims, preferred_element_type=F32)
+
+
+def kernel(
+    S,
+    T,
+    gh_ref,
+    gw_ref,
+    gain_ref,
+    patches_hbm,
+    grads_hbm,
+    w_hbm,
+    proj_hbm,
+    pg_ref,
+    qg_ref,
+    patches,
+    grads,
+    w,
+    proj,
+    picked,
+    xg,
+    nrm,
+    nrmf,
+    nst,
+    nall,
+    gcall,
+    hps,
+    hpr,
+    outr,
+    ret,
+    load_sem,
+    s1s,
+    s1r,
+    s2s,
+    s2r,
+    n1s,
+    n1r,
+    n2s,
+    n2r,
+    gzs,
+    gzr,
+    gys,
+    gyr,
+    hs,
+    hr,
+    rs,
+    rr,
+):
+    s = lax.axis_index("seq")
+    t = lax.axis_index("tp")
+    rows = grads.shape[0]
+    feat = grads.shape[1]
+    slot = rows // S
+    quart = rows // T
+    wide = T * feat
+    nslice = wide // S
+    per_block = S // T
+    Z = S // 2
+    z = s // 2
+    y = lax.rem(s, 2)
+    t_core = t + 1 - 2 * lax.rem(t, 2)
+    t_x = lax.rem(t + 2, T)
+    t_far = t_core + 2 - 4 * (t_core // 2)
+    s_y = s + 1 - 2 * y
+
+    loads = [
+        pltpu.make_async_copy(a, b, load_sem.at[i])
+        for i, (a, b) in enumerate(
+            ((patches_hbm, patches), (grads_hbm, grads), (w_hbm, w), (proj_hbm, proj))
+        )
+    ]
+    for c in loads:
+        c.start()
+
+    def seq_peer(k):
+        return lax.rem(s + k, S)
+
+    def seq_from(k):
+        return lax.rem(s + S - k, S)
+
+    barrier = pltpu.get_barrier_semaphore()
+    for k in range(1, S):
+        pl.semaphore_signal(barrier, inc=1, device_id=(seq_peer(k), t), device_id_type=MESH)
+    for k in range(1, T):
+        pl.semaphore_signal(barrier, inc=1, device_id=(s, lax.rem(t + k, T)), device_id_type=MESH)
+
+    starts = []
+    total = jnp.int32(0)
+    first_here = jnp.int32(0)
+    sizes = []
+    for i in range(3 * S):
+        if i % 3 == 0:
+            starts.append(total)
+            first_here = jnp.where(s == i // 3, total, first_here)
+        size = gh_ref[i] * gw_ref[i]
+        sizes.append(size)
+        total = total + size
+    starts.append(total)
+    end0 = first_here
+    end1 = first_here
+    end2 = first_here
+    for d in range(S):
+        here = s == d
+        end0 = jnp.where(here, starts[d] + sizes[3 * d], end0)
+        end1 = jnp.where(here, starts[d] + sizes[3 * d] + sizes[3 * d + 1], end1)
+        end2 = jnp.where(here, starts[d + 1], end2)
+
+    def local_row(shape, dim):
+        r = lax.broadcasted_iota(jnp.int32, shape, dim)
+        d_of = r // slot
+        j = r - d_of * slot
+        lead = jnp.zeros(shape, jnp.int32)
+        end = jnp.zeros(shape, jnp.int32)
+        for d in range(S):
+            lead = jnp.where(d_of == d, (starts[d] - s + S - 1) // S, lead)
+            end = jnp.where(d_of == d, starts[d + 1], end)
+        row = lead + j
+        return jnp.where((row * S + s < end) & (row < rows), row, -1)
+
+    def arrival(shape, dim):
+        r = lax.broadcasted_iota(jnp.int32, shape, dim)
+        o = r // slot
+        j = r - o * slot
+        g = ((first_here - o + S - 1) // S + j) * S + o
+        alive = g < end2
+        key = jnp.where(g >= end0, 1, 0) + jnp.where(g >= end1, 1, 0)
+        return jnp.where(alive, key, 3 + r), alive
+
+    lrow = local_row((rows, 1), 0)
+    sel4 = jnp.where(
+        lax.broadcasted_iota(jnp.int32, (rows, 4 * rows), 1) // 4 == lrow, 0.25, 0.0
+    ).astype(BF)
+    sel1 = jnp.where(lax.broadcasted_iota(jnp.int32, (rows, rows), 1) == lrow, 1.0, 0.0).astype(BF)
+    loads[0].wait()
+    picked[0] = mm(sel4, patches[...]).astype(BF)
+    loads[1].wait()
+    picked[1] = mm(sel1, grads[...]).astype(BF)
+
+    pl.semaphore_wait(barrier, S + T - 2)
+
+    def rc(src, dst, ss, rsem, dev):
+        return pltpu.make_async_remote_copy(
+            src_ref=src,
+            dst_ref=dst,
+            send_sem=ss,
+            recv_sem=rsem,
+            device_id=dev,
+            device_id_type=MESH,
+        )
+
+    def rows_at(i, n):
+        return pl.ds(pl.multiple_of(i * n, n), n)
+
+    pending = []
+
+    def send(*a):
+        c = rc(*a)
+        c.start()
+        pending.append(c)
+
+    for k in range(1, S):
+        d = seq_peer(k)
+        send(
+            picked.at[:, rows_at(d, slot), :],
+            xg.at[t, :, rows_at(s, slot), :],
+            s1s.at[k],
+            s1r.at[k],
+            (d, t),
+        )
+    xg[t, :, rows_at(s, slot), :] = picked[:, rows_at(s, slot), :]
+    key_r, live = arrival((rows, 1), 0)
+    key_c, _ = arrival((1, rows), 1)
+    same = key_r == key_c
+    for k in range(1, S):
+        o = seq_from(k)
+        rc(
+            picked.at[:, rows_at(o, slot), :],
+            xg.at[t, :, rows_at(o, slot), :],
+            s1s.at[k],
+            s1r.at[k],
+            (o, t),
+        ).wait_recv()
+    for i in range(2):
+        send(xg.at[t, i], xg.at[t, i], s2s.at[0, i], s2r.at[0, i], (s, t_x))
+        send(xg.at[t, i], xg.at[t, i], s2s.at[1, i], s2r.at[1, i], (s, t_core))
+    for i in range(2):
+        rc(xg.at[t_x, i], xg.at[t_x, i], s2s.at[0, i], s2r.at[0, i], (s, t_x)).wait_recv()
+        send(xg.at[t_x, i], xg.at[t_x, i], s2s.at[2, i], s2r.at[2, i], (s, t_core))
+
+    def wait_rest(i):
+        rc(xg.at[t_core, i], xg.at[t_core, i], s2s.at[1, i], s2r.at[1, i], (s, t_core)).wait_recv()
+        rc(xg.at[t_far, i], xg.at[t_far, i], s2s.at[2, i], s2r.at[2, i], (s, t_core)).wait_recv()
+
+    wait_rest(0)
+    square = jnp.zeros((rows, 1), F32)
+    for b in range(T):
+        v = xg[b, 0].astype(F32)
+        square = square + jnp.sum(v * v, axis=1, keepdims=True)
+    inv = lax.rsqrt(square * (1.0 / wide) + norm_eps)
+    for b in range(T):
+        v = xg[b, 0].astype(F32) * inv * gain_ref[b]
+        nrm[b] = v.astype(BF)
+        nrmf[b] = v
+    for d in range(S):
+        off = (d % per_block) * nslice
+        part = nrmf[d // per_block, rows_at(t, quart), :]
+        nst[d] = part[:, off : off + nslice].astype(BF)
+    for k in range(1, S):
+        d = seq_peer(k)
+        send(nst.at[d], nall.at[s, rows_at(t, quart), :], n1s.at[k], n1r.at[k], (d, t))
+    nall[s, rows_at(t, quart), :] = nst[s]
+
+    loads[2].wait()
+    packed = jnp.zeros((rows, w.shape[1]), F32)
+    for b in range(T):
+        packed = packed + mm(nrm[b], w[b * feat : (b + 1) * feat, :])
+    loads[3].wait()
+    wait_rest(1)
+    heads_grad = jnp.zeros((rows, proj.shape[0]), F32)
+    for b in range(T):
+        heads_grad = heads_grad + mm(xg[b, 1], proj[:, b * feat : (b + 1) * feat], NT)
+
+    head_count = w.shape[1] // (3 * HEAD_SIZE)
+    scale = HEAD_SIZE ** (-0.5)
+    cols = []
+    for h in range(head_count):
+        q, kk, v = (
+            packed[:, (3 * h + i) * HEAD_SIZE : (3 * h + i + 1) * HEAD_SIZE].astype(BF)
+            for i in range(3)
+        )
+        gh = heads_grad[:, h * HEAD_SIZE : (h + 1) * HEAD_SIZE].astype(BF)
+        capped = jnp.tanh(mm(q, kk, NT) * (scale / soft_cap))
+        raised = jnp.where(same, jnp.exp(soft_cap * capped), 0.0)
+        prob = raised / jnp.sum(raised, axis=1, keepdims=True)
+        gp = mm(gh, v, NT)
+        gs = prob * (gp - jnp.sum(prob * gp, axis=1, keepdims=True))
+        gl = (gs * (1.0 - capped * capped)).astype(BF)
+        cols.append(mm(gl, kk) * scale)
+        cols.append(mm(gl, q, TN) * scale)
+        cols.append(mm(prob.astype(BF), gh, TN))
+    grad_f = jnp.concatenate(cols, axis=1)
+    grad_cols = grad_f.astype(BF)
+    gcall[s] = grad_cols
+    for k in range(1, Z):
+        send(gcall.at[s], gcall.at[s], gzs.at[k], gzr.at[k], (2 * lax.rem(z + k, Z) + y, t))
+    send(gcall.at[s], gcall.at[s], gys.at[0], gyr.at[0], (s_y, t))
+
+    row_dot = jnp.sum(grad_cols.astype(F32) * packed, axis=1, keepdims=True)
+    lanes = hps.shape[2]
+    dot_tile = jnp.broadcast_to(row_dot, (rows, lanes - feat))
+
+    def head_part(b):
+        part = mm(grad_cols, w[pl.ds(pl.multiple_of(b * feat, 16), feat), :], NT)
+        return jnp.concatenate([part, dot_tile], axis=1)
+
+    for i, b in enumerate((t_x, t_far, t_core)):
+        hps[i] = head_part(b).astype(BF)
+        send(hps.at[i], hpr.at[i], hs.at[i], hr.at[i], (s, b))
+    own_part = head_part(t)
+
+    for k in range(1, S):
+        o = seq_from(k)
+        rc(nst.at[o], nall.at[o, rows_at(t, quart), :], n1s.at[k], n1r.at[k], (o, t)).wait_recv()
+
+    def nq(b):
+        return nall.at[:, rows_at(b, quart), :]
+
+    send(nq(t), nq(t), n2s.at[0], n2r.at[0], (s, t_x))
+    send(nq(t), nq(t), n2s.at[1], n2r.at[1], (s, t_core))
+
+    def forward(k):
+        src = 2 * lax.rem(z + Z - k, Z) + y
+        rc(gcall.at[src], gcall.at[src], gzs.at[k], gzr.at[k], (src, t)).wait_recv()
+        send(gcall.at[src], gcall.at[src], gys.at[k], gyr.at[k], (s_y, t))
+
+    for i, b in enumerate((t_x, t_far, t_core)):
+        rc(hps.at[i], hpr.at[i], hs.at[i], hr.at[i], (s, b)).wait_recv()
+        own_part = own_part + hpr[i].astype(F32)
+    scaled = own_part[:, :feat] * gain_ref[t]
+    mean = own_part[:, feat : feat + 1] * (1.0 / wide)
+    unit = xg[t, 0].astype(F32) * inv
+    grad_rows = inv * (scaled - unit * mean) + xg[t, 1].astype(F32)
+    outr[...] = jnp.where(live, grad_rows, 0.0).astype(BF)
+    for k in range(1, S):
+        d = seq_peer(k)
+        send(
+            outr.at[rows_at(d, slot), :], ret.at[rows_at(s, slot), :], rs.at[k], rr.at[k], (d, t)
+        )
+    ret[rows_at(s, slot), :] = outr[rows_at(s, slot), :]
+
+    rc(nq(t_x), nq(t_x), n2s.at[0], n2r.at[0], (s, t_x)).wait_recv()
+    send(nq(t_x), nq(t_x), n2s.at[2], n2r.at[2], (s, t_core))
+    for k in range(1, Z):
+        forward(k)
+
+    lcol = local_row((1, rows), 1)
+    back = jnp.where(
+        lax.broadcasted_iota(jnp.int32, (4 * rows, rows), 0) // 4 == lcol, 0.25, 0.0
+    ).astype(BF)
+    for k in range(1, S):
+        o = seq_from(k)
+        rc(
+            outr.at[rows_at(o, slot), :], ret.at[rows_at(o, slot), :], rs.at[k], rr.at[k], (o, t)
+        ).wait_recv()
+    pg_ref[...] = mm(back, ret[...]).astype(BF)
+
+    rc(nq(t_core), nq(t_core), n2s.at[1], n2r.at[1], (s, t_core)).wait_recv()
+    rc(nq(t_far), nq(t_far), n2s.at[2], n2r.at[2], (s, t_core)).wait_recv()
+
+    for k in range(Z):
+        src = 2 * lax.rem(z + Z - k, Z) + 1 - y
+        rc(gcall.at[src], gcall.at[src], gys.at[k], gyr.at[k], (s_y, t)).wait_recv()
+    acc = jnp.zeros(qg_ref.shape, F32)
+    for o in range(S):
+        acc = acc + mm(nall[o], gcall[o], TN)
+    qg_ref[...] = acc * (rows * S) ** (-0.5)
+    for c in pending:
+        c.wait_send()
+
+
+def fused(S, T, patches, grad_merged, norm_gain, qkv_weight, proj_weight, grid_height, grid_width):
+    rows, feat = grad_merged.shape
+    cols = qkv_weight.shape[1]
+    slot = rows // S
+    quart = rows // T
+    nslice = T * feat // S
+    lanes = feat // 128 * 128 + 128
+    Z = S // 2
+    vm, sem = pltpu.VMEM, pltpu.SemaphoreType.DMA
+    return pl.pallas_call(
+        functools.partial(kernel, S, T),
+        out_shape=(
+            jax.ShapeDtypeStruct(patches.shape, BF),
+            jax.ShapeDtypeStruct((nslice, cols), F32),
+        ),
+        in_specs=[pl.BlockSpec(memory_space=pltpu.SMEM)] * 2
+        + [pl.BlockSpec(memory_space=pltpu.VMEM)]
+        + [pl.BlockSpec(memory_space=pl.ANY)] * 4,
+        out_specs=[pl.BlockSpec(memory_space=pltpu.VMEM)] * 2,
+        scratch_shapes=[
+            vm(patches.shape, BF),
+            vm((rows, feat), BF),
+            vm(qkv_weight.shape, BF),
+            vm(proj_weight.shape, BF),
+            vm((2, rows, feat), BF),
+            vm((T, 2, rows, feat), BF),
+            vm((T, rows, feat), BF),
+            vm((T, rows, feat), F32),
+            vm((S, quart, nslice), BF),
+            vm((S, rows, nslice), BF),
+            vm((S, rows, cols), BF),
+            vm((T - 1, rows, lanes), BF),
+            vm((T - 1, rows, lanes), BF),
+            vm((rows, feat), BF),
+            vm((rows, feat), BF),
+            sem((4,)),
+            sem((S,)),
+            sem((S,)),
+            sem((3, 2)),
+            sem((3, 2)),
+            sem((S,)),
+            sem((S,)),
+            sem((3,)),
+            sem((3,)),
+            sem((Z,)),
+            sem((Z,)),
+            sem((Z,)),
+            sem((Z,)),
+            sem((T - 1,)),
+            sem((T - 1,)),
+            sem((S,)),
+            sem((S,)),
+        ],
+        compiler_params=pltpu.CompilerParams(
+            collective_id=0, has_side_effects=True, vmem_limit_bytes=40 * 1024 * 1024
+        ),
+        cost_estimate=pl.CostEstimate(flops=1 << 30, bytes_accessed=5 << 20, transcendentals=1 << 16),
+    )(
+        grid_height,
+        grid_width,
+        norm_gain.reshape(T, 1, feat),
+        patches,
+        grad_merged,
+        qkv_weight,
+        proj_weight,
+    )
+
+
 def solution(mesh):
     in_specs = (P("seq", "tp"), P("seq", "tp"), P(), P(None, "tp"), P("tp", None), P(), P())
     out_specs = (P("seq", "tp"), P("seq", "tp"))
-    return jax.shard_map(
-        on_device, mesh=mesh, in_specs=in_specs, out_specs=out_specs, check_vma=False
-    )
+    S, T = mesh.shape["seq"], mesh.shape["tp"]
+
+    def body(*args):
+        rows = args[1].shape[0]
+        slot = rows // S
+        if T == 4 and S % 2 == 0 and S <= 16 and rows % S == 0 and slot % 16 == 0:
+            return fused(S, T, *args)
+        return on_device(*args)
+
+    return jax.shard_map(body, mesh=mesh, in_specs=in_specs, out_specs=out_specs, check_vma=False)

time: 170 us -> 62 us (0.36)
  the two profiles are of different devices: /device:TPU:0 before, /device:TPU:24 now
where the time goes in v1:
time: 62 us; the launch traced here: 61.7 us
  Pallas kernels  50 us (81%)
  local copies, waits for them, and re-layouts  11 us (18%)
  between operations  0.68 us (1%)
    pallas_call x1, Pallas kernels, fused(): pl.pallas_call(functools.partial(kernel, S, T), out_shape=(jax.ShapeDtype...  50 us
    unnamed x12, local copies, waits for them, and re-layouts  9.24 us

profile of v1, /device:TPU:24, one launch (start us, length us, event | category | flops | bytes accessed | tf_op | source)
XLA Modules:
  0.0 61.7 jit_solution(3201710283418098991)
XLA Ops:
  0.6 0.8 %reshape.7.gain_ref = f32[4,1,416]{2,1,0:T(1,128)S(1)} reshape(f32[1664]{0:T(1024)} %param.9) | data formatting | bytes 13312 | tf_op jit(solution)/shard_map/reshape | solution.py:545
  1.4 1.0 %copy.10.grads_hbm = bf16[128,416]{1,0:T(8,128)(2,1)S(1)} copy(bf16[128,416]{0,1:T(8,128)(2,1)} %param.8) | data formatting | bytes 212992 | tf_op args[1]
  2.4 2.0 %copy.9.patches_hbm = bf16[512,416]{1,0:T(8,128)(2,1)} copy(bf16[512,416]{0,1:T(8,128)(2,1)} %param.7) | data formatting | bytes 851968 | tf_op args[0]
  4.4 0.0 copy-start.2
  4.4 0.0 copy-start.3
  4.4 3.3 %copy.11.w_hbm = bf16[1664,624]{1,0:T(8,128)(2,1)S(1)} copy(bf16[1664,624]{0,1:T(8,128)(2,1)} %param.10) | data formatting | bytes 4153344 | tf_op args[3]
  7.7 0.0 copy-done.2
  7.7 0.0 copy-done.3
  7.7 0.0 copy-start
  7.8 1.0 %copy-done = bf16[512,416]{1,0:T(8,128)(2,1)S(1)} copy-done((bf16[512,416]{1,0:T(8,128)(2,1)S(1)}, bf16[512,416]{1,0:T(8,128)(2,1)}, u32[]{:S(2)}) %copy-start) | copy-done | bytes 426008
  8.8 0.0 copy-start.1
  8.8 1.1 %copy-done.1 = bf16[208,1664]{1,0:T(8,128)(2,1)S(1)} copy-done((bf16[208,1664]{1,0:T(8,128)(2,1)S(1)}, bf16[208,1664]{1,0:T(8,128)(2,1)}, u32[]{:S(2)}) %copy-start.1) | copy-done | bytes 692248
  9.9 50.0 %shard_map.86 = (bf16[512,416]{1,0:T(8,128)(2,1)S(1)}, f32[208,624]{1,0:T(8,128)S(1)}) custom-call(s32[24]{0:T(128)S(1)} %copy-done.2, s32[24]{0:T(128)S(1)} %copy-done.3, f32[4,1,416]{2,1,0:T(1,128)S(1)} %reshape.7.gain_ref, bf16[512,416]{1,0:T(8,128)(2,1)S(1)} %copy-done, bf16[128,416]{1,0:T(8,128)(2,1)S(1)} %copy.10.grads_hbm, ...), custom_call_target="tpu_custom_call" | custom-call | flops 1073741824 | bytes 5242880 | tf_op jit(solution)/shard_map/pallas_call | solution.py:494
  59.9 0.9 %copy.12 = bf16[512,416]{0,1:T(8,128)(2,1)} copy(bf16[512,416]{1,0:T(8,128)(2,1)S(1)} %get-tuple-element.2) | data formatting | bytes 851968 | tf_op jit(solution)/shard_map/pallas_call | solution.py:494
  60.9 0.8 %copy.14 = f32[208,624]{1,0:T(8,128)} copy(f32[208,624]{1,0:T(8,128)S(1)} %get-tuple-element.7) | data formatting | bytes 1038336
Async XLA Ops:
  4.4 3.3 %copy-start.2 = (s32[24]{0:T(128)S(1)}, s32[24]{0:T(128)}, u32[]{:S(2)}) copy-start(s32[24]{0:T(128)} %gh_ref.1) | copy-start | bytes 292
  4.4 3.3 %copy-start.3 = (s32[24]{0:T(128)S(1)}, s32[24]{0:T(128)}, u32[]{:S(2)}) copy-start(s32[24]{0:T(128)} %gw_ref.1) | copy-start | bytes 292
  7.7 1.0 %copy-start = (bf16[512,416]{1,0:T(8,128)(2,1)S(1)}, bf16[512,416]{1,0:T(8,128)(2,1)}, u32[]{:S(2)}) copy-start(bf16[512,416]{1,0:T(8,128)(2,1)} %copy.9.patches_hbm) | copy-start | bytes 1277956
  8.8 1.1 %copy-start.1 = (bf16[208,1664]{1,0:T(8,128)(2,1)S(1)}, bf16[208,1664]{1,0:T(8,128)(2,1)}, u32[]{:S(2)}) copy-start(bf16[208,1664]{1,0:T(8,128)(2,1)} %proj_hbm.1) | copy-start | bytes 2076676

commit v2 on v1

--- a/solution.py
+++ b/solution.py
@@ -183,7 +183,6 @@
     proj,
     picked,
     xg,
-    nrm,
     nrmf,
     nst,
     nall,
@@ -212,8 +211,8 @@
 ):
     s = lax.axis_index("seq")
     t = lax.axis_index("tp")
-    rows = grads.shape[0]
-    feat = grads.shape[1]
+    feat, rows = grads.shape
+    half = S // 2
     slot = rows // S
     quart = rows // T
     wide = T * feat
@@ -296,9 +295,9 @@
     ).astype(BF)
     sel1 = jnp.where(lax.broadcasted_iota(jnp.int32, (rows, rows), 1) == lrow, 1.0, 0.0).astype(BF)
     loads[0].wait()
-    picked[0] = mm(sel4, patches[...]).astype(BF)
+    picked[0] = mm(sel4, patches[...], NT).astype(BF)
     loads[1].wait()
-    picked[1] = mm(sel1, grads[...]).astype(BF)
+    picked[1] = mm(sel1, grads[...], NT).astype(BF)
 
     pl.semaphore_wait(barrier, S + T - 2)
 
@@ -322,71 +321,121 @@
         c.start()
         pending.append(c)
 
-    for k in range(1, S):
-        d = seq_peer(k)
-        send(
-            picked.at[:, rows_at(d, slot), :],
-            xg.at[t, :, rows_at(s, slot), :],
-            s1s.at[k],
-            s1r.at[k],
-            (d, t),
-        )
+    side = s // half
+    place = lax.rem(s, half)
+
+    def group(g):
+        return side if g == 0 else 1 - side
+
+    def s1_peer(g, k):
+        return group(g) * half + lax.rem(place + k, half)
+
+    def s1_from(g, k):
+        return group(g) * half + lax.rem(place + half - k, half)
+
+    def xrows(b, i, g):
+        return xg.at[b, i, rows_at(group(g), half * slot), :]
+
+    for i in range(2):
+        for g in range(2):
+            for k in range(1 - g, half):
+                d = s1_peer(g, k)
+                send(
+                    picked.at[i, rows_at(d, slot), :],
+                    xg.at[t, i, rows_at(s, slot), :],
+                    s1s.at[i, g * half + k],
+                    s1r.at[i, g * half + k],
+                    (d, t),
+                )
     xg[t, :, rows_at(s, slot), :] = picked[:, rows_at(s, slot), :]
     key_r, live = arrival((rows, 1), 0)
     key_c, _ = arrival((1, rows), 1)
     same = key_r == key_c
-    for k in range(1, S):
-        o = seq_from(k)
-        rc(
-            picked.at[:, rows_at(o, slot), :],
-            xg.at[t, :, rows_at(o, slot), :],
-            s1s.at[k],
-            s1r.at[k],
-            (o, t),
-        ).wait_recv()
-    for i in range(2):
-        send(xg.at[t, i], xg.at[t, i], s2s.at[0, i], s2r.at[0, i], (s, t_x))
-        send(xg.at[t, i], xg.at[t, i], s2s.at[1, i], s2r.at[1, i], (s, t_core))
-    for i in range(2):
-        rc(xg.at[t_x, i], xg.at[t_x, i], s2s.at[0, i], s2r.at[0, i], (s, t_x)).wait_recv()
-        send(xg.at[t_x, i], xg.at[t_x, i], s2s.at[2, i], s2r.at[2, i], (s, t_core))
+
+    def pass_on(i, g):
+        for k in range(1 - g, half):
+            o = s1_from(g, k)
+            rc(
+                picked.at[i, rows_at(o, slot), :],
+                xg.at[t, i, rows_at(o, slot), :],
+                s1s.at[i, g * half + k],
+                s1r.at[i, g * half + k],
+                (o, t),
+            ).wait_recv()
+        send(xrows(t, i, g), xrows(t, i, g), s2s.at[0, i, g], s2r.at[0, i, g], (s, t_x))
+        send(xrows(t, i, g), xrows(t, i, g), s2s.at[1, i, g], s2r.at[1, i, g], (s, t_core))
+
+    def relay(i, g):
+        block = xrows(t_x, i, g)
+        rc(block, block, s2s.at[0, i, g], s2r.at[0, i, g], (s, t_x)).wait_recv()
+        send(block, block, s2s.at[2, i, g], s2r.at[2, i, g], (s, t_core))
 
     def wait_rest(i):
-        rc(xg.at[t_core, i], xg.at[t_core, i], s2s.at[1, i], s2r.at[1, i], (s, t_core)).wait_recv()
-        rc(xg.at[t_far, i], xg.at[t_far, i], s2s.at[2, i], s2r.at[2, i], (s, t_core)).wait_recv()
-
+        for g in range(2):
+            for j, b in ((1, t_core), (2, t_far)):
+                block = xrows(b, i, g)
+                rc(block, block, s2s.at[j, i, g], s2r.at[j, i, g], (s, t_core)).wait_recv()
+
+    def all_features(i):
+        return jnp.concatenate([xg[b, i].astype(F32) for b in range(T)], axis=1)
+
+    pass_on(0, 0)
+    pass_on(0, 1)
+    pass_on(1, 0)
+    relay(0, 0)
+    pass_on(1, 1)
+    relay(0, 1)
     wait_rest(0)
-    square = jnp.zeros((rows, 1), F32)
-    for b in range(T):
-        v = xg[b, 0].astype(F32)
-        square = square + jnp.sum(v * v, axis=1, keepdims=True)
-    inv = lax.rsqrt(square * (1.0 / wide) + norm_eps)
-    for b in range(T):
-        v = xg[b, 0].astype(F32) * inv * gain_ref[b]
-        nrm[b] = v.astype(BF)
-        nrmf[b] = v
+    gain = gain_ref[...]
+    x_all = all_features(0)
+    inv = lax.rsqrt(jnp.sum(x_all * x_all, axis=1, keepdims=True) * (1.0 / wide) + norm_eps)
+    normed_f = x_all * inv * gain
+    nrmf[...] = normed_f
+    normed = normed_f.astype(BF)
+    part = nrmf[rows_at(t, quart), :]
     for d in range(S):
-        off = (d % per_block) * nslice
-        part = nrmf[d // per_block, rows_at(t, quart), :]
-        nst[d] = part[:, off : off + nslice].astype(BF)
+        nst[d] = part[:, d * nslice : (d + 1) * nslice].astype(BF)
     for k in range(1, S):
         d = seq_peer(k)
         send(nst.at[d], nall.at[s, rows_at(t, quart), :], n1s.at[k], n1r.at[k], (d, t))
     nall[s, rows_at(t, quart), :] = nst[s]
+    relay(1, 0)
+    relay(1, 1)
 
     loads[2].wait()
-    packed = jnp.zeros((rows, w.shape[1]), F32)
-    for b in range(T):
-        packed = packed + mm(nrm[b], w[b * feat : (b + 1) * feat, :])
+    packed = mm(normed, w[...], NT)
     loads[3].wait()
     wait_rest(1)
-    heads_grad = jnp.zeros((rows, proj.shape[0]), F32)
-    for b in range(T):
-        heads_grad = heads_grad + mm(xg[b, 1], proj[:, b * feat : (b + 1) * feat], NT)
-
-    head_count = w.shape[1] // (3 * HEAD_SIZE)
+    heads_grad = mm(all_features(1).astype(BF), proj[...], NT)
+
+    head_count = w.shape[0] // (3 * HEAD_SIZE)
     scale = HEAD_SIZE ** (-0.5)
     cols = []
+    early = 256
+    near = [1, Z - 1] if Z > 2 else [1]
+    late = list(range(2, Z - 1))
+
+    def gpart(o, e):
+        return gcall.at[o, :, pl.ds(0, early) if e == 0 else pl.ds(early, gcall.shape[2] - early)]
+
+    def z_from(k):
+        return 2 * lax.rem(z + Z - k, Z) + y
+
+    def spread(e):
+        block = gpart(s, e)
+        for k in near + late:
+            d = 2 * lax.rem(z + k, Z) + y
+            send(block, block, gzs.at[e, k], gzr.at[e, k], (d, t))
+        send(block, block, gys.at[e, 0], gyr.at[e, 0], (s_y, t))
+
+    def forward(e, k):
+        block = gpart(z_from(k), e)
+        rc(block, block, gzs.at[e, k], gzr.at[e, k], (z_from(k), t)).wait_recv()
+        send(block, block, gys.at[e, k], gyr.at[e, k], (s_y, t))
+
+    def nq(b):
+        return nall.at[:, rows_at(b, quart), :]
+
     for h in range(head_count):
         q, kk, v = (
             packed[:, (3 * h + i) * HEAD_SIZE : (3 * h + i + 1) * HEAD_SIZE].astype(BF)
@@ -402,46 +451,48 @@
         cols.append(mm(gl, kk) * scale)
         cols.append(mm(gl, q, TN) * scale)
         cols.append(mm(prob.astype(BF), gh, TN))
+        if h == 0:
+            gcall[s, :, :early] = jnp.concatenate(cols, axis=1)[:, :early].astype(BF)
+            spread(0)
+            for k in range(1, S):
+                o = seq_from(k)
+                rc(
+                    nst.at[o], nall.at[o, rows_at(t, quart), :], n1s.at[k], n1r.at[k], (o, t)
+                ).wait_recv()
+            send(nq(t), nq(t), n2s.at[0], n2r.at[0], (s, t_x))
+            send(nq(t), nq(t), n2s.at[1], n2r.at[1], (s, t_core))
     grad_f = jnp.concatenate(cols, axis=1)
     grad_cols = grad_f.astype(BF)
-    gcall[s] = grad_cols
-    for k in range(1, Z):
-        send(gcall.at[s], gcall.at[s], gzs.at[k], gzr.at[k], (2 * lax.rem(z + k, Z) + y, t))
-    send(gcall.at[s], gcall.at[s], gys.at[0], gyr.at[0], (s_y, t))
+    spare = gcall.shape[2] - grad_f.shape[1]
+    padded = jnp.concatenate([grad_f, jnp.zeros((rows, spare), F32)], axis=1) if spare else grad_f
+    gcall[s, :, early:] = padded[:, early:].astype(BF)
+    spread(1)
 
     row_dot = jnp.sum(grad_cols.astype(F32) * packed, axis=1, keepdims=True)
-    lanes = hps.shape[2]
-    dot_tile = jnp.broadcast_to(row_dot, (rows, lanes - feat))
-
-    def head_part(b):
-        part = mm(grad_cols, w[pl.ds(pl.multiple_of(b * feat, 16), feat), :], NT)
-        return jnp.concatenate([part, dot_tile], axis=1)
-
+    dot_tile = jnp.broadcast_to(row_dot, (rows, hps.shape[2] - feat))
+    every = mm(grad_cols, w[...])
+    own_part = jnp.zeros((rows, feat), F32)
+    gain_own = jnp.zeros((1, feat), F32)
+    for b in range(T):
+        part = every[:, b * feat : (b + 1) * feat]
+        hps[b] = jnp.concatenate([part, dot_tile], axis=1).astype(BF)
+        own_part = jnp.where(t == b, part, own_part)
+        gain_own = jnp.where(t == b, gain[:, b * feat : (b + 1) * feat], gain_own)
     for i, b in enumerate((t_x, t_far, t_core)):
-        hps[i] = head_part(b).astype(BF)
-        send(hps.at[i], hpr.at[i], hs.at[i], hr.at[i], (s, b))
-    own_part = head_part(t)
-
-    for k in range(1, S):
-        o = seq_from(k)
-        rc(nst.at[o], nall.at[o, rows_at(t, quart), :], n1s.at[k], n1r.at[k], (o, t)).wait_recv()
-
-    def nq(b):
-        return nall.at[:, rows_at(b, quart), :]
-
-    send(nq(t), nq(t), n2s.at[0], n2r.at[0], (s, t_x))
-    send(nq(t), nq(t), n2s.at[1], n2r.at[1], (s, t_core))
-
-    def forward(k):
-        src = 2 * lax.rem(z + Z - k, Z) + y
-        rc(gcall.at[src], gcall.at[src], gzs.at[k], gzr.at[k], (src, t)).wait_recv()
-        send(gcall.at[src], gcall.at[src], gys.at[k], gyr.at[k], (s_y, t))
+        send(hps.at[b], hpr.at[i], hs.at[i], hr.at[i], (s, b))
+
+    rc(nq(t_x), nq(t_x), n2s.at[0], n2r.at[0], (s, t_x)).wait_recv()
+    send(nq(t_x), nq(t_x), n2s.at[2], n2r.at[2], (s, t_core))
+    for k in near:
+        forward(0, k)
 
     for i, b in enumerate((t_x, t_far, t_core)):
-        rc(hps.at[i], hpr.at[i], hs.at[i], hr.at[i], (s, b)).wait_recv()
-        own_part = own_part + hpr[i].astype(F32)
-    scaled = own_part[:, :feat] * gain_ref[t]
-    mean = own_part[:, feat : feat + 1] * (1.0 / wide)
+        rc(hps.at[b], hpr.at[i], hs.at[i], hr.at[i], (s, b)).wait_recv()
+        came = hpr[i].astype(F32)
+        own_part = own_part + came[:, :feat]
+        row_dot = row_dot + came[:, feat : feat + 1]
+    scaled = own_part * gain_own
+    mean = row_dot * (1.0 / wide)
     unit = xg[t, 0].astype(F32) * inv
     grad_rows = inv * (scaled - unit * mean) + xg[t, 1].astype(F32)
     outr[...] = jnp.where(live, grad_rows, 0.0).astype(BF)
@@ -452,31 +503,35 @@
         )
     ret[rows_at(s, slot), :] = outr[rows_at(s, slot), :]
 
-    rc(nq(t_x), nq(t_x), n2s.at[0], n2r.at[0], (s, t_x)).wait_recv()
-    send(nq(t_x), nq(t_x), n2s.at[2], n2r.at[2], (s, t_core))
-    for k in range(1, Z):
-        forward(k)
-
-    lcol = local_row((1, rows), 1)
-    back = jnp.where(
-        lax.broadcasted_iota(jnp.int32, (4 * rows, rows), 0) // 4 == lcol, 0.25, 0.0
-    ).astype(BF)
+    for k in late:
+        forward(0, k)
+    for k in near + late:
+        forward(1, k)
+
+    rc(nq(t_core), nq(t_core), n2s.at[1], n2r.at[1], (s, t_core)).wait_recv()
+    rc(nq(t_far), nq(t_far), n2s.at[2], n2r.at[2], (s, t_core)).wait_recv()
+
+    width = qg_ref.shape[1]
+
+    def term(o):
+        return mm(nall[o], gcall[o, :, :width], TN)
+
+    acc = term(s)
+    for k in near + late:
+        acc = acc + term(z_from(k))
+
     for k in range(1, S):
         o = seq_from(k)
         rc(
             outr.at[rows_at(o, slot), :], ret.at[rows_at(o, slot), :], rs.at[k], rr.at[k], (o, t)
         ).wait_recv()
-    pg_ref[...] = mm(back, ret[...]).astype(BF)
-
-    rc(nq(t_core), nq(t_core), n2s.at[1], n2r.at[1], (s, t_core)).wait_recv()
-    rc(nq(t_far), nq(t_far), n2s.at[2], n2r.at[2], (s, t_core)).wait_recv()
-
-    for k in range(Z):
-        src = 2 * lax.rem(z + Z - k, Z) + 1 - y
-        rc(gcall.at[src], gcall.at[src], gys.at[k], gyr.at[k], (s_y, t)).wait_recv()
-    acc = jnp.zeros(qg_ref.shape, F32)
-    for o in range(S):
-        acc = acc + mm(nall[o], gcall[o], TN)
+    pg_ref[...] = mm(ret[...], sel4, TN).astype(BF)
+
+    for k in [0] + near + late:
+        src = z_from(k) + 1 - 2 * y
+        for e in range(2):
+            rc(gpart(src, e), gpart(src, e), gys.at[e, k], gyr.at[e, k], (s_y, t)).wait_recv()
+        acc = acc + term(src)
     qg_ref[...] = acc * (rows * S) ** (-0.5)
     for c in pending:
         c.wait_send()
@@ -491,10 +546,10 @@
     lanes = feat // 128 * 128 + 128
     Z = S // 2
     vm, sem = pltpu.VMEM, pltpu.SemaphoreType.DMA
-    return pl.pallas_call(
+    patch_t, qkv_grad = pl.pallas_call(
         functools.partial(kernel, S, T),
         out_shape=(
-            jax.ShapeDtypeStruct(patches.shape, BF),
+            jax.ShapeDtypeStruct((feat, 4 * rows), BF),
             jax.ShapeDtypeStruct((nslice, cols), F32),
         ),
         in_specs=[pl.BlockSpec(memory_space=pltpu.SMEM)] * 2
@@ -502,52 +557,52 @@
         + [pl.BlockSpec(memory_space=pl.ANY)] * 4,
         out_specs=[pl.BlockSpec(memory_space=pltpu.VMEM)] * 2,
         scratch_shapes=[
-            vm(patches.shape, BF),
-            vm((rows, feat), BF),
-            vm(qkv_weight.shape, BF),
+            vm((feat, 4 * rows), BF),
+            vm((feat, rows), BF),
+            vm((cols, T * feat), BF),
             vm(proj_weight.shape, BF),
             vm((2, rows, feat), BF),
             vm((T, 2, rows, feat), BF),
-            vm((T, rows, feat), BF),
-            vm((T, rows, feat), F32),
+            vm((rows, T * feat), F32),
             vm((S, quart, nslice), BF),
             vm((S, rows, nslice), BF),
-            vm((S, rows, cols), BF),
-            vm((T - 1, rows, lanes), BF),
+            vm((S, rows, -(-cols // 128) * 128), BF),
+            vm((T, rows, lanes), BF),
             vm((T - 1, rows, lanes), BF),
             vm((rows, feat), BF),
             vm((rows, feat), BF),
             sem((4,)),
-            sem((S,)),
-            sem((S,)),
-            sem((3, 2)),
-            sem((3, 2)),
+            sem((2, S)),
+            sem((2, S)),
+            sem((3, 2, 2)),
+            sem((3, 2, 2)),
             sem((S,)),
             sem((S,)),
             sem((3,)),
             sem((3,)),
-            sem((Z,)),
-            sem((Z,)),
-            sem((Z,)),
-            sem((Z,)),
+            sem((2, Z)),
+            sem((2, Z)),
+            sem((2, Z)),
+            sem((2, Z)),
             sem((T - 1,)),
             sem((T - 1,)),
             sem((S,)),
             sem((S,)),
         ],
         compiler_params=pltpu.CompilerParams(
-            collective_id=0, has_side_effects=True, vmem_limit_bytes=40 * 1024 * 1024
+            collective_id=0, has_side_effects=True, vmem_limit_bytes=56 * 1024 * 1024
         ),
         cost_estimate=pl.CostEstimate(flops=1 << 30, bytes_accessed=5 << 20, transcendentals=1 << 16),
     )(
         grid_height,
         grid_width,
-        norm_gain.reshape(T, 1, feat),
-        patches,
-        grad_merged,
-        qkv_weight,
+        norm_gain.reshape(1, T * feat),
+        patches.T,
+        grad_merged.T,
+        qkv_weight.T,
         proj_weight,
     )
+    return patch_t.T, qkv_grad
 
 
 def solution(mesh):

time: 62 us -> 51.8 us (0.84)
  the two profiles are of different devices: /device:TPU:24 before, /device:TPU:0 now
where the time goes in v2:
time: 51.8 us; the launch traced here: 51.5 us
  Pallas kernels  45.9 us (89%)
  local copies, waits for them, and re-layouts  4.96 us (10%)
  between operations  0.64 us (1%)
    pallas_call x1, Pallas kernels, fused(): pl.pallas_call(functools.partial(kernel, S, T), out_shape=(jax.ShapeDtype...  45.9 us
    unnamed x2, local copies, waits for them, and re-layouts  3.67 us
    reshape x1, local copies, waits for them, and re-layouts, fused(): norm_gain.reshape(1, T * feat)  1.3 us

profile of v2, /device:TPU:0, one launch (start us, length us, event | category | flops | bytes accessed | tf_op | source)
XLA Modules:
  0.0 51.5 jit_solution(9201047826902148166)
XLA Ops:
  0.6 1.3 %reshape.7.gain_ref = f32[1,1664]{1,0:T(1,128)} reshape(f32[1664]{0:T(1024)} %param.9) | data formatting | bytes 13312 | tf_op jit(solution)/shard_map/reshape | solution.py:599
  1.9 45.9 %shard_map.86 = (bf16[416,512]{1,0:T(8,128)(2,1)}, f32[208,624]{1,0:T(8,128)}) custom-call(s32[24]{0:T(128)} %gh_ref.1, s32[24]{0:T(128)} %gw_ref.1, f32[1,1664]{1,0:T(1,128)} %reshape.7.gain_ref, bf16[416,512]{1,0:T(8,128)(2,1)} %bitcast.6, bf16[416,128]{1,0:T(8,128)(2,1)} %bitcast.7, bf16[624,1664]{1,0:T(8,128)(2,1)} %bitcast.5, bf16[208,1664]{1,0:T(8,128)(2,1)} %proj_hbm.1), custom_call_target="tpu_custom_call" | custom-call | flops 1073741824 | bytes 5242880 | tf_op jit(solution)/shard_map/pallas_call | solution.py:549
  47.9 1.8 %copy.11 = bf16[512,416]{0,1:T(8,128)(2,1)} copy(bf16[512,416]{0,1:T(8,128)(2,1)} %bitcast.4) | data formatting | bytes 851968
  49.7 1.9 %copy.12 = f32[208,624]{1,0:T(8,128)} copy(f32[208,624]{1,0:T(8,128)} %get-tuple-element.9) | data formatting | bytes 1038336

commit v3 on v2

--- a/solution.py
+++ b/solution.py
@@ -189,6 +189,7 @@
     gcall,
     hps,
     hpr,
+    hsum,
     outr,
     ret,
     load_sem,
@@ -386,7 +387,7 @@
     pass_on(1, 1)
     relay(0, 1)
     wait_rest(0)
-    gain = gain_ref[...]
+    gain = gain_ref[...].reshape(1, wide)
     x_all = all_features(0)
     inv = lax.rsqrt(jnp.sum(x_all * x_all, axis=1, keepdims=True) * (1.0 / wide) + norm_eps)
     normed_f = x_all * inv * gain
@@ -403,20 +404,20 @@
     relay(1, 1)
 
     loads[2].wait()
-    packed = mm(normed, w[...], NT)
+    packed = mm(w[...], normed, NT)
     loads[3].wait()
     wait_rest(1)
-    heads_grad = mm(all_features(1).astype(BF), proj[...], NT)
+    heads_grad = mm(proj[...], all_features(1).astype(BF), NT)
 
     head_count = w.shape[0] // (3 * HEAD_SIZE)
     scale = HEAD_SIZE ** (-0.5)
     cols = []
-    early = 256
+    early = 3 * HEAD_SIZE // 16 * 16
     near = [1, Z - 1] if Z > 2 else [1]
     late = list(range(2, Z - 1))
 
     def gpart(o, e):
-        return gcall.at[o, :, pl.ds(0, early) if e == 0 else pl.ds(early, gcall.shape[2] - early)]
+        return gcall.at[o, pl.ds(0, early) if e == 0 else pl.ds(early, gcall.shape[1] - early), :]
 
     def z_from(k):
         return 2 * lax.rem(z + Z - k, Z) + y
@@ -438,56 +439,57 @@
 
     for h in range(head_count):
         q, kk, v = (
-            packed[:, (3 * h + i) * HEAD_SIZE : (3 * h + i + 1) * HEAD_SIZE].astype(BF)
+            packed[(3 * h + i) * HEAD_SIZE : (3 * h + i + 1) * HEAD_SIZE].astype(BF)
             for i in range(3)
         )
-        gh = heads_grad[:, h * HEAD_SIZE : (h + 1) * HEAD_SIZE].astype(BF)
-        capped = jnp.tanh(mm(q, kk, NT) * (scale / soft_cap))
+        gh = heads_grad[h * HEAD_SIZE : (h + 1) * HEAD_SIZE].astype(BF)
+        capped = jnp.tanh(mm(q, kk, TN) * (scale / soft_cap))
         raised = jnp.where(same, jnp.exp(soft_cap * capped), 0.0)
         prob = raised / jnp.sum(raised, axis=1, keepdims=True)
-        gp = mm(gh, v, NT)
+        gp = mm(gh, v, TN)
         gs = prob * (gp - jnp.sum(prob * gp, axis=1, keepdims=True))
         gl = (gs * (1.0 - capped * capped)).astype(BF)
-        cols.append(mm(gl, kk) * scale)
-        cols.append(mm(gl, q, TN) * scale)
-        cols.append(mm(prob.astype(BF), gh, TN))
+        cols.append(mm(kk, gl, NT) * scale)
+        cols.append(mm(q, gl) * scale)
+        cols.append(mm(gh, prob.astype(BF)))
         if h == 0:
-            gcall[s, :, :early] = jnp.concatenate(cols, axis=1)[:, :early].astype(BF)
+            gcall[s, :early, :] = jnp.concatenate(cols, axis=0)[:early].astype(BF)
             spread(0)
-            for k in range(1, S):
-                o = seq_from(k)
-                rc(
-                    nst.at[o], nall.at[o, rows_at(t, quart), :], n1s.at[k], n1r.at[k], (o, t)
-                ).wait_recv()
-            send(nq(t), nq(t), n2s.at[0], n2r.at[0], (s, t_x))
-            send(nq(t), nq(t), n2s.at[1], n2r.at[1], (s, t_core))
-    grad_f = jnp.concatenate(cols, axis=1)
+    grad_f = jnp.concatenate(cols, axis=0)
     grad_cols = grad_f.astype(BF)
-    spare = gcall.shape[2] - grad_f.shape[1]
-    padded = jnp.concatenate([grad_f, jnp.zeros((rows, spare), F32)], axis=1) if spare else grad_f
-    gcall[s, :, early:] = padded[:, early:].astype(BF)
+    gcall[s, early:, :] = grad_cols[early:]
     spread(1)
 
-    row_dot = jnp.sum(grad_cols.astype(F32) * packed, axis=1, keepdims=True)
-    dot_tile = jnp.broadcast_to(row_dot, (rows, hps.shape[2] - feat))
-    every = mm(grad_cols, w[...])
+    product = (grad_cols.astype(F32) * packed).astype(BF)
+    dot_tile = mm(product, jnp.ones((product.shape[0], hps.shape[2] - feat), BF), TN)
+    row_dot = dot_tile[:, :1]
+    every = mm(grad_cols, w[...], TN)
     own_part = jnp.zeros((rows, feat), F32)
     gain_own = jnp.zeros((1, feat), F32)
+    across = jnp.zeros((rows, hps.shape[2]), F32)
     for b in range(T):
         part = every[:, b * feat : (b + 1) * feat]
-        hps[b] = jnp.concatenate([part, dot_tile], axis=1).astype(BF)
+        block = jnp.concatenate([part, dot_tile], axis=1)
+        hps[b] = block.astype(BF)
+        across = jnp.where(t_x == b, block, across)
         own_part = jnp.where(t == b, part, own_part)
         gain_own = jnp.where(t == b, gain[:, b * feat : (b + 1) * feat], gain_own)
-    for i, b in enumerate((t_x, t_far, t_core)):
-        send(hps.at[b], hpr.at[i], hs.at[i], hr.at[i], (s, b))
-
-    rc(nq(t_x), nq(t_x), n2s.at[0], n2r.at[0], (s, t_x)).wait_recv()
-    send(nq(t_x), nq(t_x), n2s.at[2], n2r.at[2], (s, t_core))
+    send(hps.at[t_far], hpr.at[1], hs.at[1], hr.at[1], (s, t_core))
+    send(hps.at[t_core], hpr.at[0], hs.at[0], hr.at[0], (s, t_core))
+    rc(hps.at[t_far], hpr.at[1], hs.at[1], hr.at[1], (s, t_core)).wait_recv()
+    hsum[...] = (across + hpr[1].astype(F32)).astype(BF)
+    send(hsum, hpr.at[2], hs.at[2], hr.at[2], (s, t_x))
+
+    for k in range(1, S):
+        o = seq_from(k)
+        rc(nst.at[o], nall.at[o, rows_at(t, quart), :], n1s.at[k], n1r.at[k], (o, t)).wait_recv()
+    send(nq(t), nq(t), n2s.at[0], n2r.at[0], (s, t_x))
+    send(nq(t), nq(t), n2s.at[1], n2r.at[1], (s, t_core))
     for k in near:
         forward(0, k)
 
-    for i, b in enumerate((t_x, t_far, t_core)):
-        rc(hps.at[b], hpr.at[i], hs.at[i], hr.at[i], (s, b)).wait_recv()
+    for i, b in ((0, t_core), (2, t_x)):
+        rc(hsum, hpr.at[i], hs.at[i], hr.at[i], (s, b)).wait_recv()
         came = hpr[i].astype(F32)
         own_part = own_part + came[:, :feat]
         row_dot = row_dot + came[:, feat : feat + 1]
@@ -505,16 +507,18 @@
 
     for k in late:
         forward(0, k)
-    for k in near + late:
+    for k in near:
+        forward(1, k)
+    rc(nq(t_x), nq(t_x), n2s.at[0], n2r.at[0], (s, t_x)).wait_recv()
+    send(nq(t_x), nq(t_x), n2s.at[2], n2r.at[2], (s, t_core))
+    for k in late:
         forward(1, k)
 
     rc(nq(t_core), nq(t_core), n2s.at[1], n2r.at[1], (s, t_core)).wait_recv()
     rc(nq(t_far), nq(t_far), n2s.at[2], n2r.at[2], (s, t_core)).wait_recv()
 
-    width = qg_ref.shape[1]
-
     def term(o):
-        return mm(nall[o], gcall[o, :, :width], TN)
+        return mm(gcall[o], nall[o])
 
     acc = term(s)
     for k in near + late:
@@ -546,11 +550,11 @@
     lanes = feat // 128 * 128 + 128
     Z = S // 2
     vm, sem = pltpu.VMEM, pltpu.SemaphoreType.DMA
-    patch_t, qkv_grad = pl.pallas_call(
+    patch_t, grad_t = pl.pallas_call(
         functools.partial(kernel, S, T),
         out_shape=(
             jax.ShapeDtypeStruct((feat, 4 * rows), BF),
-            jax.ShapeDtypeStruct((nslice, cols), F32),
+            jax.ShapeDtypeStruct((cols, nslice), F32),
         ),
         in_specs=[pl.BlockSpec(memory_space=pltpu.SMEM)] * 2
         + [pl.BlockSpec(memory_space=pltpu.VMEM)]
@@ -566,9 +570,10 @@
             vm((rows, T * feat), F32),
             vm((S, quart, nslice), BF),
             vm((S, rows, nslice), BF),
-            vm((S, rows, -(-cols // 128) * 128), BF),
+            vm((S, cols, rows), BF),
             vm((T, rows, lanes), BF),
             vm((T - 1, rows, lanes), BF),
+            vm((rows, lanes), BF),
             vm((rows, feat), BF),
             vm((rows, feat), BF),
             sem((4,)),
@@ -596,13 +601,13 @@
     )(
         grid_height,
         grid_width,
-        norm_gain.reshape(1, T * feat),
+        norm_gain,
         patches.T,
         grad_merged.T,
         qkv_weight.T,
         proj_weight,
     )
-    return patch_t.T, qkv_grad
+    return patch_t.T, grad_t.T
 
 
 def solution(mesh):

time: 51.8 us -> 49 us (0.946)
  Pallas kernels: 45.9 us -> 44.2 us
  local copies, waits for them, and re-layouts: 4.96 us -> 3.89 us
    pallas_call x1, Pallas kernels: 45.9 us -> 44.2 us  [fused(): pl.pallas_call(functools.partial(kernel, S, T), out_shape=(jax.ShapeDtype...]
    reshape x1 -> x0, local copies, waits for them, and re-layouts: 1.3 us -> none  [fused(): norm_gain.reshape(1, T * feat)]
where the time goes in v3:
time: 49 us; the launch traced here: 48.8 us
  Pallas kernels  44.2 us (90%)
  local copies, waits for them, and re-layouts  3.89 us (8%)
  between operations  0.64 us (1%)
    pallas_call x1, Pallas kernels, fused(): pl.pallas_call(functools.partial(kernel, S, T), out_shape=(jax.ShapeDtype...  44.2 us
    unnamed x2, local copies, waits for them, and re-layouts  3.89 us

profile of v3, /device:TPU:0, one launch (start us, length us, event | category | flops | bytes accessed | tf_op | source)
XLA Modules:
  0.0 48.8 jit_solution(15417208344161774164)
XLA Ops:
  0.6 44.2 %shard_map.86 = (bf16[416,512]{1,0:T(8,128)(2,1)}, f32[624,208]{1,0:T(8,128)}) custom-call(s32[24]{0:T(128)} %gh_ref.1, s32[24]{0:T(128)} %gw_ref.1, f32[1664]{0:T(1024)} %gain_ref.1, bf16[416,512]{1,0:T(8,128)(2,1)} %bitcast.8, bf16[416,128]{1,0:T(8,128)(2,1)} %bitcast.9, bf16[624,1664]{1,0:T(8,128)(2,1)} %bitcast.7, bf16[208,1664]{1,0:T(8,128)(2,1)} %proj_hbm.1), custom_call_target="tpu_custom_call" | custom-call | flops 1073741824 | bytes 5242880 | tf_op jit(solution)/shard_map/pallas_call | solution.py:553
  44.9 2.1 %copy.9 = f32[208,624]{1,0:T(8,128)} copy(f32[208,624]{0,1:T(8,128)} %bitcast.5) | data formatting | bytes 1038336
  47.0 1.8 %copy.11 = bf16[512,416]{0,1:T(8,128)(2,1)} copy(bf16[512,416]{0,1:T(8,128)(2,1)} %bitcast.6) | data formatting | bytes 851968
